TPU v7x, 32 devices: a whole 2x2x4 slice. The times are simulated.
32 devices in a mesh: dom: 8 (over z, x), face: 4 (over y, core).
Axes of the slice: x: 2, y: 2, z: 4, core: 2. Of those that a mesh axis runs over, the one named last changes fastest.
Arguments:
- elem_state: bfloat16 [256, 320], P(('dom', 'face')), may hold values from -6 to 6
- face_metric: bfloat16 [1024, 320], P(('dom', 'face')), may hold values from 0.5 to 2
- right_side: float32 [256, 320], P(('dom', 'face'))
- block_inverse: bfloat16 [256, 320, 320], P(('dom', 'face')), as said below
- trace_basis: bfloat16 [320, 320], replicated, may hold values from -0.3125 to 0.3125
- flux_basis: bfloat16 [320, 320], replicated, may hold values from -0.3125 to 0.3125
- face_rows: int32 [1024], P(('dom', 'face')), may hold values from 0 to 7
- face_cols: int32 [1024], P(('dom', 'face')), may hold values from 0 to 31
- face_counts: int32 [32], P(('dom', 'face')), may hold values from 1 to 32, as said below
Outputs:
- solution: float32 [256, 320], P(('dom', 'face'))
- residual: float32 [256, 320], P(('dom', 'face'))
Inputs may be any that keep to these rules, and one draw needn't show every extreme that they name: The first face_counts[p] slots of device p are live, the others are not; some device has all 32 slots live. `block_inverse`: each block is a diagonal part with entries between 0.5 and 1 plus a dense part whose entries, those on the diagonal included, are of order 320 ** -0.5 or smaller.
All inputs are finite; a program needn't handle non-finite values.
Results may differ from a plain program's by a relative error of at most 0.0044.
Values may be sent and summed in bfloat16 or wider, within the bound.
A program may use at most 64 MiB of HBM per device.

v0:
```python
import jax
import jax.numpy as jnp
from jax import lax
from jax.sharding import PartitionSpec as P


def shifted(array, axis, by):
    peers = lax.axis_size(axis)
    return lax.ppermute(array, axis, [(i, (i + by) % peers) for i in range(peers)])


def coupled_sum(use_blocks, use_rows, use_cols, vectors):
    picked = jnp.dot(use_cols, vectors, preferred_element_type=jnp.float32).astype(jnp.bfloat16)
    products = jnp.einsum("fij,fj->fi", use_blocks, picked, preferred_element_type=jnp.float32)
    return jnp.dot(use_rows.astype(jnp.float32), products, precision=lax.Precision.HIGHEST)


def on_device(
    elem_state,
    face_metric,
    right_side,
    block_inverse,
    trace_basis,
    flux_basis,
    face_rows,
    face_cols,
    face_counts,
):
    slot_count = face_rows.shape[0]
    owned_rows = right_side.shape[0]
    group_state = lax.all_gather(elem_state, "face", axis=0, tiled=True)
    members = group_state.shape[0]
    upwind_pick = (face_cols[:, None] == jnp.arange(members, dtype=jnp.int32)[None, :]).astype(
        jnp.bfloat16
    )
    upwind = jnp.dot(upwind_pick, group_state, preferred_element_type=jnp.float32)
    speeds = 1.0 + 0.5 * jnp.tanh(upwind)
    live_mask = (jnp.arange(slot_count, dtype=jnp.int32) < face_counts[0]).astype(jnp.float32)
    scaled = (trace_basis.astype(jnp.float32)[None, :, :] * speeds[:, None, :]).astype(jnp.bfloat16)
    inner_prod = jnp.einsum("fik,kj->fij", scaled, flux_basis, preferred_element_type=jnp.float32)
    weighted = (
        inner_prod * (face_metric.astype(jnp.float32) * live_mask[:, None])[:, None, :]
    ).astype(jnp.bfloat16)
    blocks = jnp.einsum(
        "fik,jk->fij", weighted, trace_basis, preferred_element_type=jnp.float32
    ).astype(jnp.bfloat16)
    row_pick = (face_rows[None, :] == jnp.arange(owned_rows, dtype=jnp.int32)[:, None]).astype(
        jnp.bfloat16
    )

    def operate(vector):
        group_vec = lax.all_gather(vector.astype(jnp.bfloat16), "face", axis=0, tiled=True)
        summed = shifted(coupled_sum(blocks, row_pick, upwind_pick, group_vec), "dom", 1)
        return vector + jnp.einsum(
            "eij,ej->ei",
            block_inverse,
            summed.astype(jnp.bfloat16),
            preferred_element_type=jnp.float32,
        )

    start_vec = jnp.einsum(
        "eij,ej->ei",
        block_inverse,
        right_side.astype(jnp.bfloat16),
        preferred_element_type=jnp.float32,
    )
    first_vec = operate(start_vec)
    norm_first, proj_first = lax.psum(
        (jnp.sum(first_vec * first_vec), jnp.sum(start_vec * first_vec)), ("dom", "face")
    )
    second_vec = operate(first_vec)
    cross_term, norm_second, proj_second = lax.psum(
        (
            jnp.sum(first_vec * second_vec),
            jnp.sum(second_vec * second_vec),
            jnp.sum(start_vec * second_vec),
        ),
        ("dom", "face"),
    )
    ridge = 0.001 * (norm_first + norm_second)
    determinant = (norm_first + ridge) * (norm_second + ridge) - cross_term * cross_term
    coef_first = (proj_first * (norm_second + ridge) - proj_second * cross_term) / determinant
    coef_second = (proj_second * (norm_first + ridge) - proj_first * cross_term) / determinant
    solution = coef_first * start_vec + coef_second * first_vec
    residual = start_vec - coef_first * first_vec - coef_second * second_vec
    return (solution, residual)


def solution(mesh):
    return jax.shard_map(
        on_device,
        mesh=mesh,
        in_specs=(
            P(("dom", "face"), None),
            P(("dom", "face"), None),
            P(("dom", "face"), None),
            P(("dom", "face"), None, None),
            P(),
            P(),
            P(("dom", "face")),
            P(("dom", "face")),
            P(("dom", "face")),
        ),
        out_specs=(P(("dom", "face"), None), P(("dom", "face"), None)),
        check_vma=False,
    )
```

profile of v0, /device:TPU:0, one launch (start us, length us, event | category | flops | bytes accessed | tf_op | source)
XLA Modules:
  0.0 104.9 jit_solution(16633414108953105683)
XLA Ops:
  0.6 0.0 copy-start
  1.4 6.4 %all_gather.9 = bf16[32,320]{1,0:T(8,128)(2,1)S(1)} all-gather(bf16[8,320]{1,0:T(8,128)(2,1)} %param.9), channel_id=1, replica_groups=mesh['dom'=8,'face'=4] {'face'}, dimensions={0}, use_global_device_ids=true | all-gather | bytes 25600 | tf_op jit(solution)/shard_map/all_gather | solution.py:31
  7.9 1.0 convert_element_type.48
  8.9 0.7 convert_bitcast_fusion.2
  9.6 0.0 copy-done
  9.6 0.6 fusion.27
  10.2 5.4 %all_gather.10 = bf16[32,320]{1,0:T(8,128)(2,1)S(1)} all-gather(bf16[8,320]{1,0:T(8,128)(2,1)S(1)} %bitcast.67), channel_id=1, replica_groups=mesh['dom'=8,'face'=4] {'face'}, dimensions={0}, use_global_device_ids=true | all-gather | bytes 25600 | tf_op jit(solution)/shard_map/all_gather | solution.py:52
  15.6 0.9 fusion.3
  16.5 0.8 fusion.4
  17.3 0.8 convert_multiply_fusion
  18.1 12.8 %convolution_convert_fusion = bf16[32,320,320]{2,1,0:T(8,128)(2,1)} fusion(f32[32,320]{1,0:T(8,128)S(1)} %convert_multiply_fusion, f32[32,320]{1,0:T(8,128)S(1)} %fusion.3, f32[320,320]{1,0:T(8,128)S(1)} %convert_element_type.48, bf16[320,320]{1,0:T(8,128)(2,1)} %param.13, bf16[320,320]{1,0:T(8,128)(2,1)} %param.14), kind=kOutput, calls=%fused_computation.4 | convolution fusion | flops 4210688000 | bytes 7454720 | tf_op jit(solution)/shard_map/fik,jk->fij/dot_general | solution.py:44
  30.9 0.0 copy-start.2
  30.9 0.0 copy-start.3
  30.9 0.0 copy-start.1
  31.0 5.6 %fusion.17 = f32[32,1,320]{2,1,0:T(1,128)S(1)} fusion(bf16[32,320,320]{2,1,0:T(8,128)(2,1)} %convolution_convert_fusion, bf16[32,320,1]{1,0,2:T(8,128)(2,1)S(1)} %fusion.4), kind=kOutput, calls=%fused_computation.22 | convolution fusion | flops 6553600 | bytes 6615040 | tf_op jit(solution)/shard_map/fij,fj->fi/dot_general | solution.py:14
  36.6 0.0 copy-done.2
  36.6 0.2 fusion.11
  36.7 1.7 %collective-permute-start = (bf16[8,320]{1,0:T(8,128)(2,1)S(1)}, bf16[8,320]{1,0:T(8,128)(2,1)S(1)}, u32[]{:S(2)}, u32[]{:S(2)}) collective-permute-start(bf16[8,320]{1,0:T(8,128)(2,1)S(1)} %fusion.11), channel_id=1, source_target_pairs={{0,4},{4,8},{8,12},{12,16},{16,20},{20,24},{24,28},{28,0},{1,5},{5... | collective-permute-start | bytes 15368 | tf_op jit(solution)/shard_map/ppermute | solution.py:9
  38.5 4.6 %collective-permute-done = bf16[8,320]{1,0:T(8,128)(2,1)S(1)} collective-permute-done((bf16[8,320]{1,0:T(8,128)(2,1)S(1)}, bf16[8,320]{1,0:T(8,128)(2,1)S(1)}, u32[]{:S(2)}, u32[]{:S(2)}) %collective-permute-start) | collective-permute-done | bytes 5152 | tf_op jit(solution)/shard_map/ppermute | solution.py:9
  43.1 0.6 fusion.25
  43.8 5.2 %all_gather.11 = bf16[32,320]{1,0:T(8,128)(2,1)S(1)} all-gather(bf16[8,320]{1,0:T(8,128)(2,1)S(1)} %get-tuple-element.12), channel_id=1, replica_groups=mesh['dom'=8,'face'=4] {'face'}, dimensions={0}, use_global_device_ids=true | all-gather | bytes 25600 | tf_op jit(solution)/shard_map/all_gather | solution.py:52
  48.9 0.0 copy-done.3
  49.0 0.2 fusion.5
  49.1 0.0 copy-done.1
  49.1 2.3 %fusion.14 = f32[32,1,320]{2,1,0:T(1,128)S(1)} fusion(bf16[32,320,320]{2,1,0:T(8,128)(2,1)S(1)} %copy-done.1, bf16[32,320,1]{1,0,2:T(8,128)(2,1)S(1)} %fusion.5), kind=kOutput, calls=%fused_computation.19 | convolution fusion | flops 6553600 | bytes 6615040 | tf_op jit(solution)/shard_map/fij,fj->fi/dot_general | solution.py:14
  51.4 0.2 fusion.9
  51.6 0.0 collective-permute-start.1
  51.6 6.3 %collective-permute-done.1 = bf16[8,320]{1,0:T(8,128)(2,1)S(1)} collective-permute-done((bf16[8,320]{1,0:T(8,128)(2,1)S(1)}, bf16[8,320]{1,0:T(8,128)(2,1)S(1)}, u32[]{:S(2)}, u32[]{:S(2)}) %collective-permute-start.1) | collective-permute-done | bytes 5152 | tf_op jit(solution)/shard_map/ppermute | solution.py:9
  57.9 0.6 fusion.23
  58.5 0.7 multiply_reduce_fusion
  59.2 37.4 %all-reduce = (f32[]{:T(128)}, f32[]{:T(128)}, f32[]{:T(128)}, f32[]{:T(128)}, f32[]{:T(128)}) all-reduce(f32[]{:T(128)} %get-tuple-element.3, f32[]{:T(128)} %get-tuple-element.6, f32[]{:T(128)} %get-tuple-element.5, f32[]{:T(128)} %get-tuple-element.4, f32[]{:T(128)} %get-tuple-element.2), channel_id=1, replica_groups=mesh['dom'=8,'face'=4] {'dom','face'}, use_global_device_ids=true, to_apply=%region_7.0 | all-reduce | flops 5 | bytes 40 | tf_op jit(solution)/shard_map/psum | solution.py:72
  104.3 0.6 fusion.22
  (3 shorter events, 0.0 us)
Async XLA Ops:
  0.6 8.9 %copy-start = (bf16[8,320,320]{2,1,0:T(8,128)(2,1)S(1)}, bf16[8,320,320]{2,1,0:T(8,128)(2,1)}, u32[]{:S(2)}) copy-start(bf16[8,320,320]{2,1,0:T(8,128)(2,1)} %param.12) | copy-start | bytes 4915204
  30.9 5.6 %copy-start.2 = (s32[32]{0:T(128)S(1)}, s32[32]{0:T(128)}, u32[]{:S(2)}) copy-start(s32[32]{0:T(128)} %param.15) | copy-start | bytes 388
  30.9 18.0 %copy-start.3 = (s32[32]{0:T(128)S(1)}, s32[32]{0:T(128)}, u32[]{:S(2)}) copy-start(s32[32]{0:T(128)} %param.16) | copy-start | bytes 388
  30.9 18.2 %copy-start.1 = (bf16[32,320,320]{2,1,0:T(8,128)(2,1)S(1)}, bf16[32,320,320]{2,1,0:T(8,128)(2,1)}, u32[]{:S(2)}) copy-start(bf16[32,320,320]{2,1,0:T(8,128)(2,1)} %convolution_convert_fusion) | copy-start | bytes 19660804
  36.7 6.4 %collective-permute-start = (bf16[8,320]{1,0:T(8,128)(2,1)S(1)}, bf16[8,320]{1,0:T(8,128)(2,1)S(1)}, u32[]{:S(2)}, u32[]{:S(2)}) collective-permute-start(bf16[8,320]{1,0:T(8,128)(2,1)S(1)} %fusion.11), channel_id=1, source_target_pairs={{0,4},{4,8},{8,12},{12,16},{16,20},{20,24},{24,28},{28,0},{1,5},{5... | collective-permute-start | bytes 15368 | tf_op jit(solution)/shard_map/ppermute | solution.py:9
  51.6 6.3 %collective-permute-start.1 = (bf16[8,320]{1,0:T(8,128)(2,1)S(1)}, bf16[8,320]{1,0:T(8,128)(2,1)S(1)}, u32[]{:S(2)}, u32[]{:S(2)}) collective-permute-start(bf16[8,320]{1,0:T(8,128)(2,1)S(1)} %fusion.9), channel_id=1, source_target_pairs={{0,4},{4,8},{8,12},{12,16},{16,20},{20,24},{24,28},{28,0},{1,5},{5... | collective-permute-start | bytes 15368 | tf_op jit(solution)/shard_map/ppermute | solution.py:9
where the time goes:
time: 106 us; the launch traced here: 105 us
  blocking collectives  54.4 us (51%)
  matrix products  24.8 us (23%)
  waiting for transfers between devices  11 us (10%)
  between operations  9.14 us (9%)
  other arithmetic  3.84 us (4%)
  starting transfers between devices  1.72 us (2%)
    psum x1, blocking collectives, on_device(): lax.psum((jnp.sum(first_vec * second_vec), jnp.sum(second_vec * second_ve...  37.4 us
    dot_general x1, matrix products, on_device(): jnp.einsum('fik,jk->fij', weighted, trace_basis, preferred_element_type=j...  12.8 us
    ppermute x2, waiting for transfers between devices, shifted(): lax.ppermute(array, axis, [(i, (i + by) % peers) for i in range(peers)])  11 us
    all_gather x2, blocking collectives, operate(): lax.all_gather(vector.astype(jnp.bfloat16), 'face', axis=0, tiled=True)  10.6 us
    dot_general x2, matrix products, coupled_sum(): jnp.einsum('fij,fj->fi', use_blocks, picked, preferred_element_type=jnp.f...  7.89 us
    all_gather x1, blocking collectives, on_device(): group_state = lax.all_gather(elem_state, 'face', axis=0, tiled=True)  6.43 us
  transfers between devices with their start and end apart: 2, of which 2 were waited for; matrix products, arithmetic and copies ran while one was open for 0% of the time, Pallas kernels for 0%

commit v1 on v0

v1 whole, which is shorter than its diff:
```python
import functools

import jax
import jax.numpy as jnp
from jax import lax
from jax.experimental import pallas as pl
from jax.experimental.pallas import tpu as pltpu
from jax.sharding import PartitionSpec as P

MESH = pl.DeviceIdType.MESH
F32 = jnp.float32
BF16 = jnp.bfloat16
LANES = 128
MAX_RADIX = 8


def radices_of(count):
    radices = []
    while count > 1:
        best = next((r for r in range(MAX_RADIX, 1, -1) if count % r == 0), None)
        if best is None:
            best = next(r for r in range(MAX_RADIX + 1, count + 1) if count % r == 0)
        radices.append(best)
        count //= best
    return radices


def nn(a, b):
    return jnp.dot(a, b, preferred_element_type=F32)


def nt(a, b):
    return lax.dot_general(a, b, (((1,), (1,)), ((), ())), preferred_element_type=F32)


def tn(a, b):
    return lax.dot_general(a, b, (((0,), (0,)), ((), ())), preferred_element_type=F32)


def two_terms(x):
    high = x.astype(BF16).astype(F32)
    return jnp.concatenate([high, x - high], axis=0).astype(BF16)


def kernel(
    n_dom,
    n_face,
    state_ref,
    metric_ref,
    rhs_ref,
    binv_hbm,
    trace_hbm,
    flux_hbm,
    rows_ref,
    cols_ref,
    count_ref,
    sol_ref,
    res_ref,
    binv,
    trace,
    flux,
    state_out,
    meta_out,
    state_in,
    metric_in,
    meta_in,
    vec_out,
    vec_in,
    sums_out,
    sums_in,
    load_sem,
    state_send,
    state_recv,
    setup_send,
    setup_recv,
    vec_send,
    vec_recv,
    sums_send,
    sums_recv,
):
    d = lax.axis_index("dom")
    f = lax.axis_index("face")
    ahead = lax.rem(d + 1, n_dom)
    behind = lax.rem(d + n_dom - 1, n_dom)
    own, nv = rhs_ref.shape
    slots = metric_ref.shape[0]
    members = own * n_face

    loads = [
        pltpu.make_async_copy(binv_hbm.at[e], binv.at[e], load_sem.at[e]) for e in range(own)
    ]
    load_trace = pltpu.make_async_copy(trace_hbm, trace, load_sem.at[own])
    load_flux = pltpu.make_async_copy(flux_hbm, flux, load_sem.at[own + 1])
    for load in loads:
        load.start()
    load_trace.start()
    load_flux.start()

    stages = []
    stages.append(
        (n_face, f, [(d, lax.rem(f + j, n_face)) for j in range(1, n_face)])
    )
    stride = 1
    for radix in radices_of(n_dom):
        digit = lax.rem(d // stride, radix)
        peers = [
            (d + (lax.rem(digit + j, radix) - digit) * stride, f) for j in range(1, radix)
        ]
        stages.append((radix, digit, peers))
        stride *= radix

    barrier = pltpu.get_barrier_semaphore()
    greeted = 0
    for peer in range(n_face):
        for dom in (ahead, behind):
            pl.semaphore_signal(barrier, inc=1, device_id=(dom, peer), device_id_type=MESH)
            greeted += 1
    for _, _, peers in stages:
        for peer in peers:
            pl.semaphore_signal(barrier, inc=1, device_id=peer, device_id_type=MESH)
            greeted += 1

    slot_ids = lax.broadcasted_iota(jnp.int32, (1, slots), 1)
    live_cols = jnp.where(slot_ids < count_ref[0], cols_ref[...], -1)
    meta_out[...] = jnp.zeros_like(meta_out)
    meta_out[0:1, 0:slots] = live_cols
    meta_out[1:2, 0:slots] = rows_ref[...]
    state_out[...] = state_ref[...].astype(F32)

    pl.semaphore_wait(barrier, greeted)

    sends = []
    sends.append(
        pltpu.make_async_remote_copy(
            meta_out, meta_in, setup_send.at[0], setup_recv.at[0], (ahead, f), MESH
        )
    )
    sends.append(
        pltpu.make_async_remote_copy(
            metric_ref, metric_in, setup_send.at[1], setup_recv.at[1], (ahead, f), MESH
        )
    )
    for peer in range(n_face):
        sends.append(
            pltpu.make_async_remote_copy(
                state_out, state_in.at[f], state_send.at[peer], state_recv.at[f], (ahead, peer), MESH
            )
        )
    for send in sends:
        send.start()

    row_ids = lax.broadcasted_iota(jnp.int32, (own, nv), 0)

    def precondition(vector):
        rounded = vector.astype(BF16).astype(F32)
        total = jnp.zeros((own, nv), F32)
        for e in range(own):
            total += nt(jnp.where(row_ids == e, rounded, 0.0).astype(BF16), binv[e])
        return total

    def send_vector(step, vector):
        vec_out[step] = vector
        for peer in range(n_face):
            copy = pltpu.make_async_remote_copy(
                vec_out.at[step],
                vec_in.at[step, f],
                vec_send.at[step, peer],
                vec_recv.at[step, f],
                (ahead, peer),
                MESH,
            )
            copy.start()
            sends.append(copy)

    for load in loads:
        load.wait()
    start_vec = precondition(rhs_ref[...])
    send_vector(0, start_vec)

    load_trace.wait()
    load_flux.wait()
    sends[0].wait_recv()
    sends[1].wait_recv()
    for peer in range(n_face):
        pltpu.make_async_remote_copy(
            state_out,
            state_in.at[peer],
            state_send.at[peer],
            state_recv.at[peer],
            (ahead, peer),
            MESH,
        ).wait_recv()
    member_ids = lax.broadcasted_iota(jnp.int32, (members, slots), 0)
    pick = (member_ids == meta_in[0:1, 0:slots]).astype(F32).astype(BF16)
    own_ids = lax.broadcasted_iota(jnp.int32, (own, slots), 0)
    gather_rows = (own_ids == meta_in[1:2, 0:slots]).astype(F32).astype(BF16)
    upwind = tn(pick, state_in[...].reshape(members, nv).astype(BF16))
    speeds = 1.0 + 0.5 * jnp.tanh(upwind)
    metric = metric_in[...].astype(F32)

    def operate(step, vector):
        for peer in range(n_face):
            pltpu.make_async_remote_copy(
                vec_out.at[step],
                vec_in.at[step, peer],
                vec_send.at[step, peer],
                vec_recv.at[step, peer],
                (ahead, peer),
                MESH,
            ).wait_recv()
        group = vec_in[step].reshape(members, nv).astype(BF16)
        picked = tn(pick, group).astype(BF16)
        lifted = nn(picked, trace[...]) * metric
        spread = nt(two_terms(lifted), flux[...])
        scaled = (spread[:slots] + spread[slots:]) * speeds
        high = scaled.astype(BF16)
        low = (scaled - high.astype(F32)).astype(BF16)
        summed = nn(gather_rows, high) + nn(gather_rows, low)
        back = nt(two_terms(summed), trace[...])
        return vector + precondition(back[:own] + back[own:])

    first_vec = operate(0, start_vec)
    send_vector(1, first_vec)
    second_vec = operate(1, first_vec)

    def lane_sums(x):
        row = jnp.sum(x, axis=0, keepdims=True)
        padded = -(-nv // LANES) * LANES
        row = jnp.concatenate([row, jnp.zeros((1, padded - nv), F32)], axis=1)
        return sum(row[:, at : at + LANES] for at in range(0, padded, LANES))

    partial = jnp.concatenate(
        [
            lane_sums(first_vec * first_vec),
            lane_sums(first_vec * second_vec),
            lane_sums(second_vec * second_vec),
            lane_sums(start_vec * first_vec),
            lane_sums(start_vec * second_vec),
            jnp.zeros((3, LANES), F32),
        ],
        axis=0,
    )
    base = 0
    for index, (radix, digit, peers) in enumerate(stages):
        sums_out[index] = partial
        for j, peer in enumerate(peers):
            copy = pltpu.make_async_remote_copy(
                sums_out.at[index],
                sums_in.at[base + j],
                sums_send.at[base + j],
                sums_recv.at[base + j],
                peer,
                MESH,
            )
            copy.start()
            sends.append(copy)
        for j, peer in enumerate(peers):
            pltpu.make_async_remote_copy(
                sums_out.at[index],
                sums_in.at[base + j],
                sums_send.at[base + j],
                sums_recv.at[base + j],
                peer,
                MESH,
            ).wait_recv()
            partial += sums_in[base + j]
        base += len(peers)

    totals = jnp.sum(partial, axis=1, keepdims=True)
    norm_first = totals[0:1]
    cross_term = totals[1:2]
    norm_second = totals[2:3]
    proj_first = totals[3:4]
    proj_second = totals[4:5]
    ridge = 0.001 * (norm_first + norm_second)
    determinant = (norm_first + ridge) * (norm_second + ridge) - cross_term * cross_term
    coef_first = (proj_first * (norm_second + ridge) - proj_second * cross_term) / determinant
    coef_second = (proj_second * (norm_first + ridge) - proj_first * cross_term) / determinant
    sol_ref[...] = coef_first * start_vec + coef_second * first_vec
    res_ref[...] = start_vec - coef_first * first_vec - coef_second * second_vec
    for send in sends:
        send.wait_send()


def on_device(
    n_dom,
    n_face,
    elem_state,
    face_metric,
    right_side,
    block_inverse,
    trace_basis,
    flux_basis,
    face_rows,
    face_cols,
    face_counts,
):
    own, nv = right_side.shape
    slots = face_rows.shape[0]
    radices = radices_of(n_dom)
    exchanges = n_face - 1 + sum(r - 1 for r in radices)
    dma = pltpu.SemaphoreType.DMA
    vmem = pl.BlockSpec(memory_space=pltpu.VMEM)
    smem = pl.BlockSpec(memory_space=pltpu.SMEM)
    hbm = pl.BlockSpec(memory_space=pl.ANY)
    return pl.pallas_call(
        functools.partial(kernel, n_dom, n_face),
        out_shape=(
            jax.ShapeDtypeStruct((own, nv), F32),
            jax.ShapeDtypeStruct((own, nv), F32),
        ),
        in_specs=[vmem, vmem, vmem, hbm, hbm, hbm, vmem, vmem, smem],
        out_specs=(vmem, vmem),
        scratch_shapes=[
            pltpu.VMEM((own, nv, nv), BF16),
            pltpu.VMEM((nv, nv), BF16),
            pltpu.VMEM((nv, nv), BF16),
            pltpu.VMEM((own, nv), F32),
            pltpu.VMEM((8, LANES), jnp.int32),
            pltpu.VMEM((n_face, own, nv), F32),
            pltpu.VMEM((slots, nv), BF16),
            pltpu.VMEM((8, LANES), jnp.int32),
            pltpu.VMEM((2, own, nv), F32),
            pltpu.VMEM((2, n_face, own, nv), F32),
            pltpu.VMEM((1 + len(radices), 8, LANES), F32),
            pltpu.VMEM((exchanges, 8, LANES), F32),
            dma((own + 2,)),
            dma((n_face,)),
            dma((n_face,)),
            dma((2,)),
            dma((2,)),
            dma((2, n_face)),
            dma((2, n_face)),
            dma((exchanges,)),
            dma((exchanges,)),
        ],
        compiler_params=pltpu.CompilerParams(
            collective_id=0, has_side_effects=True, vmem_limit_bytes=24 * 1024 * 1024
        ),
    )(
        elem_state,
        face_metric,
        right_side,
        block_inverse,
        trace_basis,
        flux_basis,
        face_rows.reshape(1, slots),
        face_cols.reshape(1, slots),
        face_counts,
    )


def solution(mesh):
    split = P(("dom", "face"))
    return jax.shard_map(
        functools.partial(on_device, mesh.shape["dom"], mesh.shape["face"]),
        mesh=mesh,
        in_specs=(
            P(("dom", "face"), None),
            P(("dom", "face"), None),
            P(("dom", "face"), None),
            P(("dom", "face"), None, None),
            P(),
            P(),
            split,
            split,
            split,
        ),
        out_specs=(P(("dom", "face"), None), P(("dom", "face"), None)),
        check_vma=False,
    )
```

time: 106 us -> 36.9 us (0.35)
  blocking collectives: 54.4 us -> 0 us
  Pallas kernels: 0 us -> 27.2 us
  matrix products: 24.8 us -> 0 us
  waiting for transfers between devices: 11 us -> 0 us
  local copies, waits for them, and re-layouts: 0.03 us -> 8.07 us
  between operations: 9.14 us -> 1.3 us
  other arithmetic: 3.84 us -> 0 us
  starting transfers between devices: 1.72 us -> 0 us
    psum x1 -> x0, blocking collectives: 37.4 us -> none  [on_device(): lax.psum((jnp.sum(first_vec * second_vec), jnp.sum(second_vec * second_ve...]
    pallas_call x0 -> x1, Pallas kernels: none -> 27.2 us  [on_device(): pl.pallas_call(functools.partial(kernel, n_dom, n_face), out_shape=(jax.S...]
    dot_general x11 -> x0, matrix products: 24.8 us -> none  [the longest x1 12.8 us: on_device(): jnp.einsum('fik,jk->fij', weighted, trace_basis, preferred_element_type=j...]
    all_gather x3 -> x0, blocking collectives: 17 us -> none  [the longest x2 10.6 us: operate(): lax.all_gather(vector.astype(jnp.bfloat16), 'face', axis=0, tiled=True)]
    ppermute x2 -> x0, waiting for transfers between devices: 11 us -> none  [shifted(): lax.ppermute(array, axis, [(i, (i + by) % peers) for i in range(peers)])]
    unnamed x8 -> x18, local copies, waits for them, and re-layouts: 0.02 us -> 8.07 us
    ppermute x2 -> x0, starting transfers between devices: 1.72 us -> none  [shifted(): lax.ppermute(array, axis, [(i, (i + by) % peers) for i in range(peers)])]
    convert_element_type x4 -> x0, other arithmetic: 1.7 us -> none  [the longest x1 0.98 us: on_device(): trace_basis.astype(jnp.float32)[None, :, :] * speeds[:, None, :]]
  transfers between devices with their start and end apart: 2 -> 0, of which waited for: 2 -> 0; matrix products, arithmetic and copies ran while one was open for 0% -> 0% of each run, Pallas kernels for 0% -> 0%
where the time goes in v1:
time: 36.9 us; the launch traced here: 36.5 us
  Pallas kernels  27.2 us (74%)
  local copies, waits for them, and re-layouts  8.07 us (22%)
  between operations  1.3 us (4%)
    pallas_call x1, Pallas kernels, on_device(): pl.pallas_call(functools.partial(kernel, n_dom, n_face), out_shape=(jax.S...  27.2 us
    unnamed x18, local copies, waits for them, and re-layouts  8.07 us

profile of v1, /device:TPU:0, one launch (start us, length us, event | category | flops | bytes accessed | tf_op | source)
XLA Modules:
  0.0 36.5 jit_solution(12841639980667730395)
XLA Ops:
  1.3 0.0 copy-start
  1.3 1.5 %copy-done = bf16[8,320,320]{2,1,0:T(8,128)(2,1)S(1)} copy-done((bf16[8,320,320]{2,1,0:T(8,128)(2,1)S(1)}, bf16[8,320,320]{2,1,0:T(8,128)(2,1)}, u32[]{:S(2)}) %copy-start) | copy-done | bytes 1638424
  2.8 0.0 copy-start.1
  2.8 0.9 %copy-done.1 = bf16[320,320]{1,0:T(8,128)(2,1)S(1)} copy-done((bf16[320,320]{1,0:T(8,128)(2,1)S(1)}, bf16[320,320]{1,0:T(8,128)(2,1)}, u32[]{:S(2)}) %copy-start.1) | copy-done | bytes 204824
  3.8 0.0 copy-start.2
  3.8 0.9 %copy-done.2 = bf16[320,320]{1,0:T(8,128)(2,1)S(1)} copy-done((bf16[320,320]{1,0:T(8,128)(2,1)S(1)}, bf16[320,320]{1,0:T(8,128)(2,1)}, u32[]{:S(2)}) %copy-start.2) | copy-done | bytes 204824
  4.7 0.0 copy-start.3
  4.7 0.7 %copy-done.3 = bf16[32,320]{1,0:T(8,128)(2,1)S(1)} copy-done((bf16[32,320]{1,0:T(8,128)(2,1)S(1)}, bf16[32,320]{1,0:T(8,128)(2,1)}, u32[]{:S(2)}) %copy-start.3) | copy-done | bytes 20504
  5.5 0.0 copy-start.4
  5.5 0.7 %copy-done.4 = f32[8,320]{1,0:T(8,128)S(1)} copy-done((f32[8,320]{1,0:T(8,128)S(1)}, f32[8,320]{1,0:T(8,128)}, u32[]{:S(2)}) %copy-start.4) | copy-done | bytes 10264
  6.2 0.0 copy-start.5
  6.2 0.7 %copy-done.5 = bf16[8,320]{1,0:T(8,128)(2,1)S(1)} copy-done((bf16[8,320]{1,0:T(8,128)(2,1)S(1)}, bf16[8,320]{1,0:T(8,128)(2,1)}, u32[]{:S(2)}) %copy-start.5) | copy-done | bytes 5144
  6.9 0.0 copy-start.6
  6.9 0.7 %copy-done.6 = s32[32]{0:T(128)S(1)} copy-done((s32[32]{0:T(128)S(1)}, s32[32]{0:T(128)}, u32[]{:S(2)}) %copy-start.6) | copy-done | bytes 152
  7.5 0.0 copy-start.7
  7.5 0.7 %copy-done.7 = s32[32]{0:T(128)S(1)} copy-done((s32[32]{0:T(128)S(1)}, s32[32]{0:T(128)}, u32[]{:S(2)}) %copy-start.7) | copy-done | bytes 152
  8.2 27.2 %shard_map.104 = (f32[8,320]{1,0:T(8,128)S(1)}, f32[8,320]{1,0:T(8,128)S(1)}) custom-call(bf16[8,320]{1,0:T(8,128)(2,1)S(1)} %copy-done.5, bf16[32,320]{1,0:T(8,128)(2,1)S(1)} %copy-done.3, f32[8,320]{1,0:T(8,128)S(1)} %copy-done.4, bf16[8,320,320]{2,1,0:T(8,128)(2,1)S(1)} %copy-done, bf16[320,320]{1,0:T(8,128)(2,1)S(1)} %copy-done.1, ...), custom_call_target="tpu_custom_call" | custom-call | tf_op jit(solution)/shard_map/pallas_call | solution.py:306
  35.3 0.6 %copy.14 = f32[8,320]{1,0:T(8,128)} copy(f32[8,320]{1,0:T(8,128)S(1)} %get-tuple-element.4) | data formatting | bytes 20480
  35.9 0.6 %copy.15 = f32[8,320]{1,0:T(8,128)} copy(f32[8,320]{1,0:T(8,128)S(1)} %get-tuple-element.5) | data formatting | bytes 20480
Async XLA Ops:
  1.3 1.5 %copy-start = (bf16[8,320,320]{2,1,0:T(8,128)(2,1)S(1)}, bf16[8,320,320]{2,1,0:T(8,128)(2,1)}, u32[]{:S(2)}) copy-start(bf16[8,320,320]{2,1,0:T(8,128)(2,1)} %binv_hbm.1) | copy-start | bytes 4915204
  2.8 0.9 %copy-start.1 = (bf16[320,320]{1,0:T(8,128)(2,1)S(1)}, bf16[320,320]{1,0:T(8,128)(2,1)}, u32[]{:S(2)}) copy-start(bf16[320,320]{1,0:T(8,128)(2,1)} %trace_hbm.1) | copy-start | bytes 614404
  3.8 0.9 %copy-start.2 = (bf16[320,320]{1,0:T(8,128)(2,1)S(1)}, bf16[320,320]{1,0:T(8,128)(2,1)}, u32[]{:S(2)}) copy-start(bf16[320,320]{1,0:T(8,128)(2,1)} %flux_hbm.1) | copy-start | bytes 614404
  4.7 0.7 %copy-start.3 = (bf16[32,320]{1,0:T(8,128)(2,1)S(1)}, bf16[32,320]{1,0:T(8,128)(2,1)}, u32[]{:S(2)}) copy-start(bf16[32,320]{1,0:T(8,128)(2,1)} %metric_ref.1) | copy-start | bytes 61444
  5.5 0.7 %copy-start.4 = (f32[8,320]{1,0:T(8,128)S(1)}, f32[8,320]{1,0:T(8,128)}, u32[]{:S(2)}) copy-start(f32[8,320]{1,0:T(8,128)} %rhs_ref.1) | copy-start | bytes 30724
  6.2 0.7 %copy-start.5 = (bf16[8,320]{1,0:T(8,128)(2,1)S(1)}, bf16[8,320]{1,0:T(8,128)(2,1)}, u32[]{:S(2)}) copy-start(bf16[8,320]{1,0:T(8,128)(2,1)} %state_ref.1) | copy-start | bytes 15364
  6.9 0.7 %copy-start.6 = (s32[32]{0:T(128)S(1)}, s32[32]{0:T(128)}, u32[]{:S(2)}) copy-start(s32[32]{0:T(128)} %param.15) | copy-start | bytes 388
  7.5 0.7 %copy-start.7 = (s32[32]{0:T(128)S(1)}, s32[32]{0:T(128)}, u32[]{:S(2)}) copy-start(s32[32]{0:T(128)} %param.16) | copy-start | bytes 388

commit v2 on v1

v2 whole, which is shorter than its diff:
```python
import functools

import jax
import jax.numpy as jnp
from jax import lax
from jax.experimental import pallas as pl
from jax.experimental.pallas import tpu as pltpu
from jax.sharding import PartitionSpec as P

MESH = pl.DeviceIdType.MESH
F32 = jnp.float32
BF16 = jnp.bfloat16
LANES = 128
MAX_RADIX = 8
PART = 256


def radices_of(count):
    radices = []
    while count > 1:
        best = next((r for r in range(MAX_RADIX, 1, -1) if count % r == 0), None)
        if best is None:
            best = next(r for r in range(MAX_RADIX + 1, count + 1) if count % r == 0)
        radices.append(best)
        count //= best
    return radices


def nn(a, b):
    return jnp.dot(a, b, preferred_element_type=F32)


def nt(a, b):
    return lax.dot_general(a, b, (((1,), (1,)), ((), ())), preferred_element_type=F32)


def tn(a, b):
    return lax.dot_general(a, b, (((0,), (0,)), ((), ())), preferred_element_type=F32)


def two_terms(x):
    high = x.astype(BF16).astype(F32)
    return jnp.concatenate([high, x - high], axis=0).astype(BF16)


def packed(x):
    right = x[:, PART:]
    right = jnp.concatenate([right, jnp.zeros((x.shape[0], 2 * PART - x.shape[1]), F32)], axis=1)
    return jnp.concatenate([x[:, :PART], right], axis=0).astype(BF16)


def await_recv(ref, send_sem, recv_sem, peer):
    pltpu.make_async_remote_copy(ref, ref, send_sem, recv_sem, peer, MESH).wait_recv()


def await_send(ref, send_sem, recv_sem, peer):
    pltpu.make_async_remote_copy(ref, ref, send_sem, recv_sem, peer, MESH).wait_send()


def kernel(
    n_dom,
    n_face,
    state_hbm,
    metric_hbm,
    rhs_hbm,
    binv_hbm,
    trace_hbm,
    flux_hbm,
    rows_hbm,
    cols_hbm,
    count_hbm,
    terms_ref,
    state,
    rhs,
    binv,
    trace,
    flux,
    rows,
    cols,
    count,
    state_out,
    state_in,
    meta_out,
    meta_in,
    metric_in,
    vec_out,
    vec_in,
    sums_out,
    sums_in,
    load_sem,
    setup_send,
    setup_recv,
    vec_send,
    vec_recv,
    sums_send,
    sums_recv,
):
    d = lax.axis_index("dom")
    f = lax.axis_index("face")
    ahead = lax.rem(d + 1, n_dom)
    behind = lax.rem(d + n_dom - 1, n_dom)
    own, nv = rhs.shape
    slots = metric_in.shape[0]

    small = [
        pltpu.make_async_copy(src, dst, load_sem.at[own + at])
        for at, (src, dst) in enumerate(
            (
                (rhs_hbm, rhs),
                (cols_hbm, cols),
                (rows_hbm, rows),
                (count_hbm, count),
                (state_hbm, state),
                (trace_hbm, trace),
                (flux_hbm, flux),
            )
        )
    ]
    loads = [
        pltpu.make_async_copy(binv_hbm.at[e], binv.at[e], load_sem.at[e]) for e in range(own)
    ]
    small[0].start()
    for load in loads:
        load.start()
    for load in small[1:]:
        load.start()

    radices = radices_of(n_dom)
    low = lax.rem(d, radices[0])
    group = n_face * radices[0]
    flat = low * n_face + f
    stages = []
    peers = []
    for j in range(1, group):
        other = lax.rem(flat + j, group)
        peers.append((d - low + other // n_face, lax.rem(other, n_face)))
    stages.append(peers)
    stride = radices[0]
    for radix in radices[1:]:
        digit = lax.rem(d // stride, radix)
        stages.append(
            [(d + (lax.rem(digit + j, radix) - digit) * stride, f) for j in range(1, radix)]
        )
        stride *= radix

    barrier = pltpu.get_barrier_semaphore()
    greeted = 0
    greet = [peer for peers in stages for peer in peers]
    if len(radices) > 1:
        greet += [(dom, peer) for peer in range(n_face) for dom in (ahead, behind)]
    for peer in greet:
        pl.semaphore_signal(barrier, inc=1, device_id=peer, device_id_type=MESH)
        greeted += 1

    row_ids = lax.broadcasted_iota(jnp.int32, (own, nv), 0)

    def precondition(vector):
        rounded = vector.astype(BF16).astype(F32)
        total = jnp.zeros((own, nv), F32)
        for e in range(own):
            total += nt(jnp.where(row_ids == e, rounded, 0.0).astype(BF16), binv[e])
        return total

    def send_vector(step):
        for peer in range(n_face):
            pltpu.make_async_remote_copy(
                vec_out.at[step],
                vec_in.at[step, f],
                vec_send.at[step],
                vec_recv.at[step],
                (ahead, peer),
                MESH,
            ).start()

    small[1].wait()
    small[2].wait()
    small[3].wait()
    small[4].wait()
    slot_ids = lax.broadcasted_iota(jnp.int32, (1, slots), 1)
    meta_out[...] = jnp.zeros_like(meta_out)
    meta_out[0:1, 0:slots] = jnp.where(slot_ids < count[...], cols[...], -1)
    meta_out[1:2, 0:slots] = rows[...]
    state_out[...] = packed(state[...].astype(F32))
    small[0].wait()
    for load in loads:
        load.wait()
    start_vec = precondition(rhs[...])
    vec_out[0] = packed(start_vec)

    pl.semaphore_wait(barrier, greeted)

    send_vector(0)
    send_meta = pltpu.make_async_remote_copy(
        meta_out, meta_in, setup_send.at[0], setup_recv.at[0], (ahead, f), MESH
    )
    send_meta.start()
    for peer in range(n_face):
        pltpu.make_async_remote_copy(
            state_out, state_in.at[f], setup_send.at[2], setup_recv.at[2], (ahead, peer), MESH
        ).start()
    send_metric = pltpu.make_async_remote_copy(
        metric_hbm, metric_in, setup_send.at[1], setup_recv.at[1], (ahead, f), MESH
    )
    send_metric.start()

    small[5].wait()
    small[6].wait()
    send_meta.wait_recv()
    own_ids = lax.broadcasted_iota(jnp.int32, (own, slots), 0)
    absent = jnp.full((own, slots), -2, jnp.int32)
    left_ids, right_ids = [], []
    for peer in range(n_face):
        left_ids += [own_ids + peer * own, absent]
        right_ids += [absent, own_ids + peer * own]
    slot_cols = meta_in[0:1, 0:slots]
    pick_left = (jnp.concatenate(left_ids, axis=0) == slot_cols).astype(F32).astype(BF16)
    pick_right = (jnp.concatenate(right_ids, axis=0) == slot_cols).astype(F32).astype(BF16)
    gather_rows = (own_ids == meta_in[1:2, 0:slots]).astype(F32).astype(BF16)

    def picked(blocks):
        stacked = blocks.reshape(n_face * 2 * own, PART)
        return tn(pick_left, stacked), tn(pick_right, stacked)[:, : nv - PART]

    def operate(step, vector):
        await_recv(vec_in.at[step], vec_send.at[step], vec_recv.at[step], (ahead, f))
        left, right = picked(vec_in[step])
        lifted = nn(left.astype(BF16), trace[0:PART]) + nn(right.astype(BF16), trace[PART:nv])
        if step == 0:
            await_recv(state_in, setup_send.at[2], setup_recv.at[2], (ahead, f))
            upwind = jnp.concatenate(picked(state_in[...]), axis=1)
            speeds.append(1.0 + 0.5 * jnp.tanh(upwind))
            send_metric.wait_recv()
        spread = nt(two_terms(lifted * metric_in[...].astype(F32)), flux[...])
        scaled = (spread[:slots] + spread[slots:]) * speeds[0]
        high = scaled.astype(BF16)
        low = (scaled - high.astype(F32)).astype(BF16)
        summed = nn(gather_rows, high) + nn(gather_rows, low)
        back = nt(two_terms(summed), trace[...])
        return vector + precondition(back[:own] + back[own:])

    speeds = []
    first_vec = operate(0, start_vec)
    vec_out[1] = packed(first_vec)
    send_vector(1)
    second_vec = operate(1, first_vec)

    lane_ids = lax.broadcasted_iota(jnp.int32, (1, LANES), 1)

    def total_at(lane, x):
        column = jnp.sum(x, axis=1, keepdims=True)
        return jnp.where(lane_ids == lane, jnp.sum(column, axis=0, keepdims=True), 0.0)

    partial = (
        total_at(0, first_vec * first_vec)
        + total_at(1, first_vec * second_vec)
        + total_at(2, second_vec * second_vec)
        + total_at(3, start_vec * first_vec)
        + total_at(4, start_vec * second_vec)
    )
    base = 0
    for index, peers in enumerate(stages):
        sums_out[index] = partial
        for j, peer in enumerate(peers):
            pltpu.make_async_remote_copy(
                sums_out.at[index],
                sums_in.at[base + j],
                sums_send.at[index],
                sums_recv.at[index],
                peer,
                MESH,
            ).start()
        landed = sums_in.at[pl.ds(base, len(peers))]
        await_recv(landed, sums_send.at[index], sums_recv.at[index], (ahead, f))
        partial += jnp.sum(sums_in[base : base + len(peers)], axis=0)
        base += len(peers)

    norm_first = partial[:, 0:1]
    cross_term = partial[:, 1:2]
    norm_second = partial[:, 2:3]
    proj_first = partial[:, 3:4]
    proj_second = partial[:, 4:5]
    ridge = 0.001 * (norm_first + norm_second)
    determinant = (norm_first + ridge) * (norm_second + ridge) - cross_term * cross_term
    coef_first = (proj_first * (norm_second + ridge) - proj_second * cross_term) / determinant
    coef_second = (proj_second * (norm_first + ridge) - proj_first * cross_term) / determinant
    terms_ref[0] = coef_first * start_vec
    terms_ref[1] = coef_second * first_vec
    terms_ref[2] = start_vec - coef_first * first_vec
    terms_ref[3] = coef_second * second_vec

    send_meta.wait_send()
    send_metric.wait_send()
    await_send(state_in, setup_send.at[2], setup_recv.at[2], (ahead, f))
    for step in range(2):
        await_send(vec_in.at[step], vec_send.at[step], vec_recv.at[step], (ahead, f))
    base = 0
    for index, peers in enumerate(stages):
        landed = sums_in.at[pl.ds(base, len(peers))]
        await_send(landed, sums_send.at[index], sums_recv.at[index], (ahead, f))
        base += len(peers)


def on_device(
    n_dom,
    n_face,
    elem_state,
    face_metric,
    right_side,
    block_inverse,
    trace_basis,
    flux_basis,
    face_rows,
    face_cols,
    face_counts,
):
    own, nv = right_side.shape
    slots = face_rows.shape[0]
    radices = radices_of(n_dom)
    exchanges = n_face * radices[0] - 1 + sum(r - 1 for r in radices[1:])
    dma = pltpu.SemaphoreType.DMA
    vmem = pl.BlockSpec(memory_space=pltpu.VMEM)
    hbm = pl.BlockSpec(memory_space=pltpu.HBM)
    terms = pl.pallas_call(
        functools.partial(kernel, n_dom, n_face),
        out_shape=jax.ShapeDtypeStruct((4, own, nv), F32),
        in_specs=[hbm] * 9,
        out_specs=vmem,
        scratch_shapes=[
            pltpu.VMEM((own, nv), BF16),
            pltpu.VMEM((own, nv), F32),
            pltpu.VMEM((own, nv, nv), BF16),
            pltpu.VMEM((nv, nv), BF16),
            pltpu.VMEM((nv, nv), BF16),
            pltpu.VMEM((1, slots), jnp.int32),
            pltpu.VMEM((1, slots), jnp.int32),
            pltpu.VMEM((1, 1), jnp.int32),
            pltpu.VMEM((2 * own, PART), BF16),
            pltpu.VMEM((n_face, 2 * own, PART), BF16),
            pltpu.VMEM((8, LANES), jnp.int32),
            pltpu.VMEM((8, LANES), jnp.int32),
            pltpu.VMEM((slots, nv), BF16),
            pltpu.VMEM((2, 2 * own, PART), BF16),
            pltpu.VMEM((2, n_face, 2 * own, PART), BF16),
            pltpu.VMEM((len(radices), 1, LANES), F32),
            pltpu.VMEM((exchanges, 1, LANES), F32),
            dma((own + 7,)),
            dma((3,)),
            dma((3,)),
            dma((2,)),
            dma((2,)),
            dma((len(radices),)),
            dma((len(radices),)),
        ],
        compiler_params=pltpu.CompilerParams(
            collective_id=0, has_side_effects=True, vmem_limit_bytes=60 * 1024 * 1024
        ),
    )(
        elem_state,
        face_metric,
        right_side,
        block_inverse,
        trace_basis,
        flux_basis,
        face_rows.reshape(1, slots),
        face_cols.reshape(1, slots),
        face_counts.reshape(1, 1),
    )
    return terms[0] + terms[1], terms[2] - terms[3]


def solution(mesh):
    split = P(("dom", "face"))
    return jax.shard_map(
        functools.partial(on_device, mesh.shape["dom"], mesh.shape["face"]),
        mesh=mesh,
        in_specs=(
            P(("dom", "face"), None),
            P(("dom", "face"), None),
            P(("dom", "face"), None),
            P(("dom", "face"), None, None),
            P(),
            P(),
            split,
            split,
            split,
        ),
        out_specs=(P(("dom", "face"), None), P(("dom", "face"), None)),
        check_vma=False,
    )
```

time: 36.9 us -> 25 us (0.68)
  local copies, waits for them, and re-layouts: 8.07 us -> 0 us
  Pallas kernels: 27.2 us -> 22.1 us
  other arithmetic: 0 us -> 1.37 us
    unnamed x18 -> x0, local copies, waits for them, and re-layouts: 8.07 us -> none
    pallas_call x1, Pallas kernels: 27.2 us -> 22.1 us  [on_device(): pl.pallas_call(functools.partial(kernel, n_dom, n_face), out_shape=jax.Sh...]
    sub x0 -> x1, other arithmetic: none -> 1.37 us  [on_device(): return (terms[0] + terms[1], terms[2] - terms[3])]
where the time goes in v2:
time: 25 us; the launch traced here: 24.8 us
  Pallas kernels  22.1 us (88%)
  other arithmetic  1.37 us (5%)
  between operations  1.29 us (5%)
    pallas_call x1, Pallas kernels, on_device(): pl.pallas_call(functools.partial(kernel, n_dom, n_face), out_shape=jax.Sh...  22.1 us
    sub x1, other arithmetic, on_device(): return (terms[0] + terms[1], terms[2] - terms[3])  1.37 us

profile of v2, /device:TPU:0, one launch (start us, length us, event | category | flops | bytes accessed | tf_op | source)
XLA Modules:
  0.0 24.8 jit_solution(10478323156396285277)
XLA Ops:
  1.3 22.1 %shard_map.104 = f32[4,8,320]{2,1,0:T(8,128)} custom-call(bf16[8,320]{1,0:T(8,128)(2,1)} %state_hbm.1, bf16[32,320]{1,0:T(8,128)(2,1)} %metric_hbm.1, f32[8,320]{1,0:T(8,128)} %rhs_hbm.1, bf16[8,320,320]{2,1,0:T(8,128)(2,1)} %binv_hbm.1, bf16[320,320]{1,0:T(8,128)(2,1)} %trace_hbm.1, bf16[320,320]{1,0:T(8,128)(2,1)} %flux_hbm.1, s32[1,32]{1,0:T(1,128)} %bitcast.8, ...), custom_call_target="tpu_custom_call" | custom-call | tf_op jit(solution)/shard_map/pallas_call | solution.py:323
  23.4 1.4 %subtract_bitcast_fusion = (f32[8,320]{1,0:T(8,128)}, f32[8,320]{1,0:T(8,128)}) fusion(f32[4,8,320]{2,1,0:T(8,128)} %shard_map.104), kind=kLoop, calls=%fused_computation | loop fusion | flops 5120 | bytes 61440 | tf_op jit(solution)/shard_map/sub | solution.py:368

commit v3 on v2

--- a/solution.py
+++ b/solution.py
@@ -73,8 +73,11 @@
     state,
     rhs,
     binv,
+    solved,
     trace,
+    trace_turned,
     flux,
+    flux_turned,
     rows,
     cols,
     count,
@@ -161,6 +164,15 @@
             total += nt(jnp.where(row_ids == e, rounded, 0.0).astype(BF16), binv[e])
         return total
 
+    def lift_and_precondition(vector):
+        high = vector.astype(BF16).astype(F32)
+        terms = jnp.concatenate([high, vector - high], axis=0)
+        term_ids = jnp.concatenate([row_ids, row_ids], axis=0)
+        total = jnp.zeros((2 * own, nv), F32)
+        for e in range(own):
+            total += nn(jnp.where(term_ids == e, terms, 0.0).astype(BF16), solved[e])
+        return total[:own] + total[own:]
+
     def send_vector(step):
         for peer in range(n_face):
             pltpu.make_async_remote_copy(
@@ -205,6 +217,11 @@
 
     small[5].wait()
     small[6].wait()
+    flux_turned[...] = flux[...].T
+    trace_turned[...] = trace[...].T
+    for e in range(own):
+        solved[e] = nt(trace_turned[...], binv[e]).astype(BF16)
+
     send_meta.wait_recv()
     own_ids = lax.broadcasted_iota(jnp.int32, (own, slots), 0)
     absent = jnp.full((own, slots), -2, jnp.int32)
@@ -215,7 +232,8 @@
     slot_cols = meta_in[0:1, 0:slots]
     pick_left = (jnp.concatenate(left_ids, axis=0) == slot_cols).astype(F32).astype(BF16)
     pick_right = (jnp.concatenate(right_ids, axis=0) == slot_cols).astype(F32).astype(BF16)
-    gather_rows = (own_ids == meta_in[1:2, 0:slots]).astype(F32).astype(BF16)
+    gather_rows = (own_ids == meta_in[1:2, 0:slots]).astype(F32)
+    gather_rows = jnp.concatenate([gather_rows, gather_rows], axis=1).astype(BF16)
 
     def picked(blocks):
         stacked = blocks.reshape(n_face * 2 * own, PART)
@@ -230,13 +248,10 @@
             upwind = jnp.concatenate(picked(state_in[...]), axis=1)
             speeds.append(1.0 + 0.5 * jnp.tanh(upwind))
             send_metric.wait_recv()
-        spread = nt(two_terms(lifted * metric_in[...].astype(F32)), flux[...])
+        spread = nn(two_terms(lifted * metric_in[...].astype(F32)), flux_turned[...])
         scaled = (spread[:slots] + spread[slots:]) * speeds[0]
-        high = scaled.astype(BF16)
-        low = (scaled - high.astype(F32)).astype(BF16)
-        summed = nn(gather_rows, high) + nn(gather_rows, low)
-        back = nt(two_terms(summed), trace[...])
-        return vector + precondition(back[:own] + back[own:])
+        summed = nn(gather_rows, two_terms(scaled))
+        return vector + lift_and_precondition(summed)
 
     speeds = []
     first_vec = operate(0, start_vec)
@@ -322,13 +337,16 @@
     hbm = pl.BlockSpec(memory_space=pltpu.HBM)
     terms = pl.pallas_call(
         functools.partial(kernel, n_dom, n_face),
-        out_shape=jax.ShapeDtypeStruct((4, own, nv), F32),
+        out_shape=pltpu.VMEM((4, own, nv), F32),
         in_specs=[hbm] * 9,
         out_specs=vmem,
         scratch_shapes=[
             pltpu.VMEM((own, nv), BF16),
             pltpu.VMEM((own, nv), F32),
             pltpu.VMEM((own, nv, nv), BF16),
+            pltpu.VMEM((own, nv, nv), BF16),
+            pltpu.VMEM((nv, nv), BF16),
+            pltpu.VMEM((nv, nv), BF16),
             pltpu.VMEM((nv, nv), BF16),
             pltpu.VMEM((nv, nv), BF16),
             pltpu.VMEM((1, slots), jnp.int32),
@@ -352,17 +370,22 @@
             dma((len(radices),)),
         ],
         compiler_params=pltpu.CompilerParams(
-            collective_id=0, has_side_effects=True, vmem_limit_bytes=60 * 1024 * 1024
+            collective_id=0, has_side_effects=True, vmem_limit_bytes=24 * 1024 * 1024
         ),
     )(
-        elem_state,
-        face_metric,
-        right_side,
-        block_inverse,
-        trace_basis,
-        flux_basis,
-        face_rows.reshape(1, slots),
-        face_cols.reshape(1, slots),
+        *(
+            pltpu.with_memory_space_constraint(operand, pltpu.HBM)
+            for operand in (
+                elem_state,
+                face_metric,
+                right_side,
+                block_inverse,
+                trace_basis,
+                flux_basis,
+                face_rows.reshape(1, slots),
+                face_cols.reshape(1, slots),
+            )
+        ),
         face_counts.reshape(1, 1),
     )
     return terms[0] + terms[1], terms[2] - terms[3]

time: 25 us -> 22.8 us (0.912)
  Pallas kernels: 22.1 us -> 20.7 us
  other arithmetic: 1.37 us -> 0.61 us
    pallas_call x1, Pallas kernels: 22.1 us -> 20.7 us  [on_device(): pl.pallas_call(functools.partial(kernel, n_dom, n_face), out_shape=pltpu....]
    sub x1, other arithmetic: 1.37 us -> 0.61 us  [on_device(): return (terms[0] + terms[1], terms[2] - terms[3])]
where the time goes in v3:
time: 22.8 us; the launch traced here: 22.6 us
  Pallas kernels  20.7 us (91%)
  between operations  1.29 us (6%)
  other arithmetic  0.61 us (3%)
    pallas_call x1, Pallas kernels, on_device(): pl.pallas_call(functools.partial(kernel, n_dom, n_face), out_shape=pltpu....  20.7 us
    sub x1, other arithmetic, on_device(): return (terms[0] + terms[1], terms[2] - terms[3])  0.61 us

profile of v3, /device:TPU:0, one launch (start us, length us, event | category | flops | bytes accessed | tf_op | source)
XLA Modules:
  0.0 22.6 jit_solution(6511216091936163593)
XLA Ops:
  1.3 20.7 %shard_map.104 = f32[4,8,320]{2,1,0:T(8,128)S(1)} custom-call(bf16[8,320]{1,0:T(8,128)(2,1)} %state_hbm.1, bf16[32,320]{1,0:T(8,128)(2,1)} %metric_hbm.1, f32[8,320]{1,0:T(8,128)} %rhs_hbm.1, bf16[8,320,320]{2,1,0:T(8,128)(2,1)} %binv_hbm.1, bf16[320,320]{1,0:T(8,128)(2,1)} %trace_hbm.1, bf16[320,320]{1,0:T(8,128)(2,1)} %flux_hbm.1, s32[1,32]{1,0:T(1,128)} %bitcast.8, ...), custom_call_target="tpu_custom_call" | custom-call | tf_op jit(solution)/shard_map/pallas_call | solution.py:338
  22.0 0.6 %subtract_bitcast_fusion = (f32[8,320]{1,0:T(8,128)}, f32[8,320]{1,0:T(8,128)}) fusion(f32[4,8,320]{2,1,0:T(8,128)S(1)} %shard_map.104), kind=kLoop, calls=%fused_computation | loop fusion | flops 5120 | bytes 61440 | tf_op jit(solution)/shard_map/sub | solution.py:391

commit v4 on v3

--- a/solution.py
+++ b/solution.py
@@ -32,10 +32,6 @@
 
 def nt(a, b):
     return lax.dot_general(a, b, (((1,), (1,)), ((), ())), preferred_element_type=F32)
-
-
-def tn(a, b):
-    return lax.dot_general(a, b, (((0,), (0,)), ((), ())), preferred_element_type=F32)
 
 
 def two_terms(x):
@@ -122,10 +118,7 @@
     loads = [
         pltpu.make_async_copy(binv_hbm.at[e], binv.at[e], load_sem.at[e]) for e in range(own)
     ]
-    small[0].start()
-    for load in loads:
-        load.start()
-    for load in small[1:]:
+    for load in small[:5] + loads + small[5:]:
         load.start()
 
     radices = radices_of(n_dom)
@@ -161,6 +154,7 @@
         rounded = vector.astype(BF16).astype(F32)
         total = jnp.zeros((own, nv), F32)
         for e in range(own):
+            loads[e].wait()
             total += nt(jnp.where(row_ids == e, rounded, 0.0).astype(BF16), binv[e])
         return total
 
@@ -193,15 +187,9 @@
     meta_out[0:1, 0:slots] = jnp.where(slot_ids < count[...], cols[...], -1)
     meta_out[1:2, 0:slots] = rows[...]
     state_out[...] = packed(state[...].astype(F32))
-    small[0].wait()
-    for load in loads:
-        load.wait()
-    start_vec = precondition(rhs[...])
-    vec_out[0] = packed(start_vec)
 
     pl.semaphore_wait(barrier, greeted)
 
-    send_vector(0)
     send_meta = pltpu.make_async_remote_copy(
         meta_out, meta_in, setup_send.at[0], setup_recv.at[0], (ahead, f), MESH
     )
@@ -215,6 +203,11 @@
     )
     send_metric.start()
 
+    small[0].wait()
+    start_vec = precondition(rhs[...])
+    vec_out[0] = packed(start_vec)
+    send_vector(0)
+
     small[5].wait()
     small[6].wait()
     flux_turned[...] = flux[...].T
@@ -230,46 +223,45 @@
         left_ids += [own_ids + peer * own, absent]
         right_ids += [absent, own_ids + peer * own]
     slot_cols = meta_in[0:1, 0:slots]
-    pick_left = (jnp.concatenate(left_ids, axis=0) == slot_cols).astype(F32).astype(BF16)
-    pick_right = (jnp.concatenate(right_ids, axis=0) == slot_cols).astype(F32).astype(BF16)
+    pick_left = (jnp.concatenate(left_ids, axis=0) == slot_cols).astype(F32)
+    pick_right = (jnp.concatenate(right_ids, axis=0) == slot_cols).astype(F32)
+    pick = jnp.concatenate([pick_left, pick_right], axis=1).T.astype(BF16)
     gather_rows = (own_ids == meta_in[1:2, 0:slots]).astype(F32)
     gather_rows = jnp.concatenate([gather_rows, gather_rows], axis=1).astype(BF16)
 
     def picked(blocks):
-        stacked = blocks.reshape(n_face * 2 * own, PART)
-        return tn(pick_left, stacked), tn(pick_right, stacked)[:, : nv - PART]
+        both = nn(pick, blocks.reshape(n_face * 2 * own, PART))
+        return both[:slots], both[slots:, : nv - PART]
+
+    await_recv(state_in, setup_send.at[2], setup_recv.at[2], (ahead, f))
+    speeds = 1.0 + 0.5 * jnp.tanh(jnp.concatenate(picked(state_in[...]), axis=1))
+    send_metric.wait_recv()
 
     def operate(step, vector):
         await_recv(vec_in.at[step], vec_send.at[step], vec_recv.at[step], (ahead, f))
         left, right = picked(vec_in[step])
         lifted = nn(left.astype(BF16), trace[0:PART]) + nn(right.astype(BF16), trace[PART:nv])
-        if step == 0:
-            await_recv(state_in, setup_send.at[2], setup_recv.at[2], (ahead, f))
-            upwind = jnp.concatenate(picked(state_in[...]), axis=1)
-            speeds.append(1.0 + 0.5 * jnp.tanh(upwind))
-            send_metric.wait_recv()
         spread = nn(two_terms(lifted * metric_in[...].astype(F32)), flux_turned[...])
-        scaled = (spread[:slots] + spread[slots:]) * speeds[0]
+        scaled = (spread[:slots] + spread[slots:]) * speeds
         summed = nn(gather_rows, two_terms(scaled))
         return vector + lift_and_precondition(summed)
 
-    speeds = []
     first_vec = operate(0, start_vec)
     vec_out[1] = packed(first_vec)
     send_vector(1)
-    second_vec = operate(1, first_vec)
-
     lane_ids = lax.broadcasted_iota(jnp.int32, (1, LANES), 1)
 
     def total_at(lane, x):
         column = jnp.sum(x, axis=1, keepdims=True)
         return jnp.where(lane_ids == lane, jnp.sum(column, axis=0, keepdims=True), 0.0)
 
+    early = total_at(0, first_vec * first_vec) + total_at(3, start_vec * first_vec)
+    second_vec = operate(1, first_vec)
+
     partial = (
-        total_at(0, first_vec * first_vec)
+        early
         + total_at(1, first_vec * second_vec)
         + total_at(2, second_vec * second_vec)
-        + total_at(3, start_vec * first_vec)
         + total_at(4, start_vec * second_vec)
     )
     base = 0

time: 22.8 us -> 22.9 us (level)
  no operation moved by 1% of the time
where the time goes in v4:
time: 22.9 us; the launch traced here: 22.7 us
  Pallas kernels  20.8 us (91%)
  between operations  1.29 us (6%)
  other arithmetic  0.61 us (3%)
    pallas_call x1, Pallas kernels, on_device(): pl.pallas_call(functools.partial(kernel, n_dom, n_face), out_shape=pltpu....  20.8 us
    sub x1, other arithmetic, on_device(): return (terms[0] + terms[1], terms[2] - terms[3])  0.61 us

profile of v4, /device:TPU:0, one launch (start us, length us, event | category | flops | bytes accessed | tf_op | source)
XLA Modules:
  0.0 22.7 jit_solution(12116240862711151305)
XLA Ops:
  1.3 20.8 %shard_map.104 = f32[4,8,320]{2,1,0:T(8,128)S(1)} custom-call(bf16[8,320]{1,0:T(8,128)(2,1)} %state_hbm.1, bf16[32,320]{1,0:T(8,128)(2,1)} %metric_hbm.1, f32[8,320]{1,0:T(8,128)} %rhs_hbm.1, bf16[8,320,320]{2,1,0:T(8,128)(2,1)} %binv_hbm.1, bf16[320,320]{1,0:T(8,128)(2,1)} %trace_hbm.1, bf16[320,320]{1,0:T(8,128)(2,1)} %flux_hbm.1, s32[1,32]{1,0:T(1,128)} %bitcast.8, ...), custom_call_target="tpu_custom_call" | custom-call | tf_op jit(solution)/shard_map/pallas_call | solution.py:330
  22.1 0.6 %subtract_bitcast_fusion = (f32[8,320]{1,0:T(8,128)}, f32[8,320]{1,0:T(8,128)}) fusion(f32[4,8,320]{2,1,0:T(8,128)S(1)} %shard_map.104), kind=kLoop, calls=%fused_computation | loop fusion | flops 5120 | bytes 61440 | tf_op jit(solution)/shard_map/sub | solution.py:383

commit v5 on v4

--- a/solution.py
+++ b/solution.py
@@ -122,17 +122,9 @@
         load.start()
 
     radices = radices_of(n_dom)
-    low = lax.rem(d, radices[0])
-    group = n_face * radices[0]
-    flat = low * n_face + f
-    stages = []
-    peers = []
-    for j in range(1, group):
-        other = lax.rem(flat + j, group)
-        peers.append((d - low + other // n_face, lax.rem(other, n_face)))
-    stages.append(peers)
-    stride = radices[0]
-    for radix in radices[1:]:
+    stages = [[(d, lax.rem(f + j, n_face)) for j in range(1, n_face)]]
+    stride = 1
+    for radix in radices:
         digit = lax.rem(d // stride, radix)
         stages.append(
             [(d + (lax.rem(digit + j, radix) - digit) * stride, f) for j in range(1, radix)]
@@ -142,8 +134,7 @@
     barrier = pltpu.get_barrier_semaphore()
     greeted = 0
     greet = [peer for peers in stages for peer in peers]
-    if len(radices) > 1:
-        greet += [(dom, peer) for peer in range(n_face) for dom in (ahead, behind)]
+    greet += [(dom, peer) for peer in range(n_face) for dom in (ahead, behind)]
     for peer in greet:
         pl.semaphore_signal(barrier, inc=1, device_id=peer, device_id_type=MESH)
         greeted += 1
@@ -323,7 +314,7 @@
     own, nv = right_side.shape
     slots = face_rows.shape[0]
     radices = radices_of(n_dom)
-    exchanges = n_face * radices[0] - 1 + sum(r - 1 for r in radices[1:])
+    exchanges = n_face - 1 + sum(r - 1 for r in radices)
     dma = pltpu.SemaphoreType.DMA
     vmem = pl.BlockSpec(memory_space=pltpu.VMEM)
     hbm = pl.BlockSpec(memory_space=pltpu.HBM)
@@ -351,15 +342,15 @@
             pltpu.VMEM((slots, nv), BF16),
             pltpu.VMEM((2, 2 * own, PART), BF16),
             pltpu.VMEM((2, n_face, 2 * own, PART), BF16),
-            pltpu.VMEM((len(radices), 1, LANES), F32),
+            pltpu.VMEM((1 + len(radices), 1, LANES), F32),
             pltpu.VMEM((exchanges, 1, LANES), F32),
             dma((own + 7,)),
             dma((3,)),
             dma((3,)),
             dma((2,)),
             dma((2,)),
-            dma((len(radices),)),
-            dma((len(radices),)),
+            dma((1 + len(radices),)),
+            dma((1 + len(radices),)),
         ],
         compiler_params=pltpu.CompilerParams(
             collective_id=0, has_side_effects=True, vmem_limit_bytes=24 * 1024 * 1024

time: 22.9 us -> 24.6 us (1.074)
  Pallas kernels: 20.8 us -> 22.6 us
    pallas_call x1, Pallas kernels: 20.8 us -> 22.6 us  [on_device(): pl.pallas_call(functools.partial(kernel, n_dom, n_face), out_shape=pltpu....]
where the time goes in v5:
time: 24.6 us; the launch traced here: 24.5 us
  Pallas kernels  22.6 us (92%)
  between operations  1.29 us (5%)
  other arithmetic  0.61 us (2%)
    pallas_call x1, Pallas kernels, on_device(): pl.pallas_call(functools.partial(kernel, n_dom, n_face), out_shape=pltpu....  22.6 us
    sub x1, other arithmetic, on_device(): return (terms[0] + terms[1], terms[2] - terms[3])  0.61 us

profile of v5, /device:TPU:0, one launch (start us, length us, event | category | flops | bytes accessed | tf_op | source)
XLA Modules:
  0.0 24.5 jit_solution(17045278867606260526)
XLA Ops:
  1.3 22.6 %shard_map.104 = f32[4,8,320]{2,1,0:T(8,128)S(1)} custom-call(bf16[8,320]{1,0:T(8,128)(2,1)} %state_hbm.1, bf16[32,320]{1,0:T(8,128)(2,1)} %metric_hbm.1, f32[8,320]{1,0:T(8,128)} %rhs_hbm.1, bf16[8,320,320]{2,1,0:T(8,128)(2,1)} %binv_hbm.1, bf16[320,320]{1,0:T(8,128)(2,1)} %trace_hbm.1, bf16[320,320]{1,0:T(8,128)(2,1)} %flux_hbm.1, s32[1,32]{1,0:T(1,128)} %bitcast.8, ...), custom_call_target="tpu_custom_call" | custom-call | tf_op jit(solution)/shard_map/pallas_call | solution.py:321
  23.8 0.6 %subtract_bitcast_fusion = (f32[8,320]{1,0:T(8,128)}, f32[8,320]{1,0:T(8,128)}) fusion(f32[4,8,320]{2,1,0:T(8,128)S(1)} %shard_map.104), kind=kLoop, calls=%fused_computation | loop fusion | flops 5120 | bytes 61440 | tf_op jit(solution)/shard_map/sub | solution.py:374

commit v6 on v4

--- a/solution.py
+++ b/solution.py
@@ -187,9 +187,13 @@
     meta_out[0:1, 0:slots] = jnp.where(slot_ids < count[...], cols[...], -1)
     meta_out[1:2, 0:slots] = rows[...]
     state_out[...] = packed(state[...].astype(F32))
+    small[0].wait()
+    start_vec = precondition(rhs[...])
+    vec_out[0] = packed(start_vec)
 
     pl.semaphore_wait(barrier, greeted)
 
+    send_vector(0)
     send_meta = pltpu.make_async_remote_copy(
         meta_out, meta_in, setup_send.at[0], setup_recv.at[0], (ahead, f), MESH
     )
@@ -202,11 +206,6 @@
         metric_hbm, metric_in, setup_send.at[1], setup_recv.at[1], (ahead, f), MESH
     )
     send_metric.start()
-
-    small[0].wait()
-    start_vec = precondition(rhs[...])
-    vec_out[0] = packed(start_vec)
-    send_vector(0)
 
     small[5].wait()
     small[6].wait()

time: 22.9 us -> 23 us (level)
  no operation moved by 1% of the time
where the time goes in v6:
time: 23 us; the launch traced here: 22.8 us
  Pallas kernels  20.9 us (91%)
  between operations  1.29 us (6%)
  other arithmetic  0.61 us (3%)
    pallas_call x1, Pallas kernels, on_device(): pl.pallas_call(functools.partial(kernel, n_dom, n_face), out_shape=pltpu....  20.9 us
    sub x1, other arithmetic, on_device(): return (terms[0] + terms[1], terms[2] - terms[3])  0.61 us

profile of v6, /device:TPU:0, one launch (start us, length us, event | category | flops | bytes accessed | tf_op | source)
XLA Modules:
  0.0 22.8 jit_solution(13405895342217939216)
XLA Ops:
  1.3 20.9 %shard_map.104 = f32[4,8,320]{2,1,0:T(8,128)S(1)} custom-call(bf16[8,320]{1,0:T(8,128)(2,1)} %state_hbm.1, bf16[32,320]{1,0:T(8,128)(2,1)} %metric_hbm.1, f32[8,320]{1,0:T(8,128)} %rhs_hbm.1, bf16[8,320,320]{2,1,0:T(8,128)(2,1)} %binv_hbm.1, bf16[320,320]{1,0:T(8,128)(2,1)} %trace_hbm.1, bf16[320,320]{1,0:T(8,128)(2,1)} %flux_hbm.1, s32[1,32]{1,0:T(1,128)} %bitcast.8, ...), custom_call_target="tpu_custom_call" | custom-call | tf_op jit(solution)/shard_map/pallas_call | solution.py:329
  22.2 0.6 %subtract_bitcast_fusion = (f32[8,320]{1,0:T(8,128)}, f32[8,320]{1,0:T(8,128)}) fusion(f32[4,8,320]{2,1,0:T(8,128)S(1)} %shard_map.104), kind=kLoop, calls=%fused_computation | loop fusion | flops 5120 | bytes 61440 | tf_op jit(solution)/shard_map/sub | solution.py:382

commit v7 on v4

--- a/solution.py
+++ b/solution.py
@@ -69,7 +69,6 @@
     state,
     rhs,
     binv,
-    solved,
     trace,
     trace_turned,
     flux,
@@ -154,18 +153,8 @@
         rounded = vector.astype(BF16).astype(F32)
         total = jnp.zeros((own, nv), F32)
         for e in range(own):
-            loads[e].wait()
             total += nt(jnp.where(row_ids == e, rounded, 0.0).astype(BF16), binv[e])
         return total
-
-    def lift_and_precondition(vector):
-        high = vector.astype(BF16).astype(F32)
-        terms = jnp.concatenate([high, vector - high], axis=0)
-        term_ids = jnp.concatenate([row_ids, row_ids], axis=0)
-        total = jnp.zeros((2 * own, nv), F32)
-        for e in range(own):
-            total += nn(jnp.where(term_ids == e, terms, 0.0).astype(BF16), solved[e])
-        return total[:own] + total[own:]
 
     def send_vector(step):
         for peer in range(n_face):
@@ -204,6 +193,8 @@
     send_metric.start()
 
     small[0].wait()
+    for load in loads:
+        load.wait()
     start_vec = precondition(rhs[...])
     vec_out[0] = packed(start_vec)
     send_vector(0)
@@ -212,8 +203,6 @@
     small[6].wait()
     flux_turned[...] = flux[...].T
     trace_turned[...] = trace[...].T
-    for e in range(own):
-        solved[e] = nt(trace_turned[...], binv[e]).astype(BF16)
 
     send_meta.wait_recv()
     own_ids = lax.broadcasted_iota(jnp.int32, (own, slots), 0)
@@ -244,7 +233,8 @@
         spread = nn(two_terms(lifted * metric_in[...].astype(F32)), flux_turned[...])
         scaled = (spread[:slots] + spread[slots:]) * speeds
         summed = nn(gather_rows, two_terms(scaled))
-        return vector + lift_and_precondition(summed)
+        back = nn(two_terms(summed), trace_turned[...])
+        return vector + precondition(back[:own] + back[own:])
 
     first_vec = operate(0, start_vec)
     vec_out[1] = packed(first_vec)
@@ -335,7 +325,6 @@
         scratch_shapes=[
             pltpu.VMEM((own, nv), BF16),
             pltpu.VMEM((own, nv), F32),
-            pltpu.VMEM((own, nv, nv), BF16),
             pltpu.VMEM((own, nv, nv), BF16),
             pltpu.VMEM((nv, nv), BF16),
             pltpu.VMEM((nv, nv), BF16),

time: 22.9 us -> 23.6 us (1.031)
  Pallas kernels: 20.8 us -> 21.6 us
    pallas_call x1, Pallas kernels: 20.8 us -> 21.6 us  [on_device(): pl.pallas_call(functools.partial(kernel, n_dom, n_face), out_shape=pltpu....]
where the time goes in v7:
time: 23.6 us; the launch traced here: 23.5 us
  Pallas kernels  21.6 us (92%)
  between operations  1.29 us (5%)
  other arithmetic  0.61 us (3%)
    pallas_call x1, Pallas kernels, on_device(): pl.pallas_call(functools.partial(kernel, n_dom, n_face), out_shape=pltpu....  21.6 us
    sub x1, other arithmetic, on_device(): return (terms[0] + terms[1], terms[2] - terms[3])  0.61 us

profile of v7, /device:TPU:0, one launch (start us, length us, event | category | flops | bytes accessed | tf_op | source)
XLA Modules:
  0.0 23.5 jit_solution(2639364092193045997)
XLA Ops:
  1.3 21.6 %shard_map.104 = f32[4,8,320]{2,1,0:T(8,128)S(1)} custom-call(bf16[8,320]{1,0:T(8,128)(2,1)} %state_hbm.1, bf16[32,320]{1,0:T(8,128)(2,1)} %metric_hbm.1, f32[8,320]{1,0:T(8,128)} %rhs_hbm.1, bf16[8,320,320]{2,1,0:T(8,128)(2,1)} %binv_hbm.1, bf16[320,320]{1,0:T(8,128)(2,1)} %trace_hbm.1, bf16[320,320]{1,0:T(8,128)(2,1)} %flux_hbm.1, s32[1,32]{1,0:T(1,128)} %bitcast.8, ...), custom_call_target="tpu_custom_call" | custom-call | tf_op jit(solution)/shard_map/pallas_call | solution.py:320
  22.9 0.6 %subtract_bitcast_fusion = (f32[8,320]{1,0:T(8,128)}, f32[8,320]{1,0:T(8,128)}) fusion(f32[4,8,320]{2,1,0:T(8,128)S(1)} %shard_map.104), kind=kLoop, calls=%fused_computation | loop fusion | flops 5120 | bytes 61440 | tf_op jit(solution)/shard_map/sub | solution.py:372

commit v8 on v4

--- a/solution.py
+++ b/solution.py
@@ -12,7 +12,6 @@
 BF16 = jnp.bfloat16
 LANES = 128
 MAX_RADIX = 8
-PART = 256
 
 
 def radices_of(count):
@@ -37,12 +36,6 @@
 def two_terms(x):
     high = x.astype(BF16).astype(F32)
     return jnp.concatenate([high, x - high], axis=0).astype(BF16)
-
-
-def packed(x):
-    right = x[:, PART:]
-    right = jnp.concatenate([right, jnp.zeros((x.shape[0], 2 * PART - x.shape[1]), F32)], axis=1)
-    return jnp.concatenate([x[:, :PART], right], axis=0).astype(BF16)
 
 
 def await_recv(ref, send_sem, recv_sem, peer):
@@ -77,7 +70,6 @@
     rows,
     cols,
     count,
-    state_out,
     state_in,
     meta_out,
     meta_in,
@@ -127,7 +119,7 @@
     flat = low * n_face + f
     stages = []
     peers = []
-    for j in range(1, group):
+    for j in range(group - 1, 0, -1):
         other = lax.rem(flat + j, group)
         peers.append((d - low + other // n_face, lax.rem(other, n_face)))
     stages.append(peers)
@@ -186,7 +178,6 @@
     meta_out[...] = jnp.zeros_like(meta_out)
     meta_out[0:1, 0:slots] = jnp.where(slot_ids < count[...], cols[...], -1)
     meta_out[1:2, 0:slots] = rows[...]
-    state_out[...] = packed(state[...].astype(F32))
 
     pl.semaphore_wait(barrier, greeted)
 
@@ -196,7 +187,7 @@
     send_meta.start()
     for peer in range(n_face):
         pltpu.make_async_remote_copy(
-            state_out, state_in.at[f], setup_send.at[2], setup_recv.at[2], (ahead, peer), MESH
+            state, state_in.at[f], setup_send.at[2], setup_recv.at[2], (ahead, peer), MESH
         ).start()
     send_metric = pltpu.make_async_remote_copy(
         metric_hbm, metric_in, setup_send.at[1], setup_recv.at[1], (ahead, f), MESH
@@ -205,7 +196,7 @@
 
     small[0].wait()
     start_vec = precondition(rhs[...])
-    vec_out[0] = packed(start_vec)
+    vec_out[0] = start_vec.astype(BF16)
     send_vector(0)
 
     small[5].wait()
@@ -217,37 +208,28 @@
 
     send_meta.wait_recv()
     own_ids = lax.broadcasted_iota(jnp.int32, (own, slots), 0)
-    absent = jnp.full((own, slots), -2, jnp.int32)
-    left_ids, right_ids = [], []
-    for peer in range(n_face):
-        left_ids += [own_ids + peer * own, absent]
-        right_ids += [absent, own_ids + peer * own]
-    slot_cols = meta_in[0:1, 0:slots]
-    pick_left = (jnp.concatenate(left_ids, axis=0) == slot_cols).astype(F32)
-    pick_right = (jnp.concatenate(right_ids, axis=0) == slot_cols).astype(F32)
-    pick = jnp.concatenate([pick_left, pick_right], axis=1).T.astype(BF16)
+    member_ids = lax.broadcasted_iota(jnp.int32, (n_face * own, slots), 0)
+    pick = (member_ids == meta_in[0:1, 0:slots]).astype(F32).T.astype(BF16)
     gather_rows = (own_ids == meta_in[1:2, 0:slots]).astype(F32)
     gather_rows = jnp.concatenate([gather_rows, gather_rows], axis=1).astype(BF16)
 
     def picked(blocks):
-        both = nn(pick, blocks.reshape(n_face * 2 * own, PART))
-        return both[:slots], both[slots:, : nv - PART]
+        return nn(pick, blocks.astype(F32).reshape(n_face * own, nv).astype(BF16))
 
     await_recv(state_in, setup_send.at[2], setup_recv.at[2], (ahead, f))
-    speeds = 1.0 + 0.5 * jnp.tanh(jnp.concatenate(picked(state_in[...]), axis=1))
+    speeds = 1.0 + 0.5 * jnp.tanh(picked(state_in[...]))
     send_metric.wait_recv()
 
     def operate(step, vector):
         await_recv(vec_in.at[step], vec_send.at[step], vec_recv.at[step], (ahead, f))
-        left, right = picked(vec_in[step])
-        lifted = nn(left.astype(BF16), trace[0:PART]) + nn(right.astype(BF16), trace[PART:nv])
+        lifted = nn(picked(vec_in[step]).astype(BF16), trace[...])
         spread = nn(two_terms(lifted * metric_in[...].astype(F32)), flux_turned[...])
         scaled = (spread[:slots] + spread[slots:]) * speeds
         summed = nn(gather_rows, two_terms(scaled))
         return vector + lift_and_precondition(summed)
 
     first_vec = operate(0, start_vec)
-    vec_out[1] = packed(first_vec)
+    vec_out[1] = first_vec.astype(BF16)
     send_vector(1)
     lane_ids = lax.broadcasted_iota(jnp.int32, (1, LANES), 1)
 
@@ -344,13 +326,12 @@
             pltpu.VMEM((1, slots), jnp.int32),
             pltpu.VMEM((1, slots), jnp.int32),
             pltpu.VMEM((1, 1), jnp.int32),
-            pltpu.VMEM((2 * own, PART), BF16),
-            pltpu.VMEM((n_face, 2 * own, PART), BF16),
+            pltpu.VMEM((n_face, own, nv), BF16),
             pltpu.VMEM((8, LANES), jnp.int32),
             pltpu.VMEM((8, LANES), jnp.int32),
             pltpu.VMEM((slots, nv), BF16),
-            pltpu.VMEM((2, 2 * own, PART), BF16),
-            pltpu.VMEM((2, n_face, 2 * own, PART), BF16),
+            pltpu.VMEM((2, own, nv), BF16),
+            pltpu.VMEM((2, n_face, own, nv), BF16),
             pltpu.VMEM((len(radices), 1, LANES), F32),
             pltpu.VMEM((exchanges, 1, LANES), F32),
             dma((own + 7,)),

time: 22.9 us -> 22.7 us (level)
  no operation moved by 1% of the time
where the time goes in v8:
time: 22.7 us; the launch traced here: 22.5 us
  Pallas kernels  20.6 us (91%)
  between operations  1.29 us (6%)
  other arithmetic  0.61 us (3%)
    pallas_call x1, Pallas kernels, on_device(): pl.pallas_call(functools.partial(kernel, n_dom, n_face), out_shape=pltpu....  20.6 us
    sub x1, other arithmetic, on_device(): return (terms[0] + terms[1], terms[2] - terms[3])  0.61 us

profile of v8, /device:TPU:0, one launch (start us, length us, event | category | flops | bytes accessed | tf_op | source)
XLA Modules:
  0.0 22.5 jit_solution(8700535044409675852)
XLA Ops:
  1.3 20.6 %shard_map.104 = f32[4,8,320]{2,1,0:T(8,128)S(1)} custom-call(bf16[8,320]{1,0:T(8,128)(2,1)} %state_hbm.1, bf16[32,320]{1,0:T(8,128)(2,1)} %metric_hbm.1, f32[8,320]{1,0:T(8,128)} %rhs_hbm.1, bf16[8,320,320]{2,1,0:T(8,128)(2,1)} %binv_hbm.1, bf16[320,320]{1,0:T(8,128)(2,1)} %trace_hbm.1, bf16[320,320]{1,0:T(8,128)(2,1)} %flux_hbm.1, s32[1,32]{1,0:T(1,128)} %bitcast.8, ...), custom_call_target="tpu_custom_call" | custom-call | tf_op jit(solution)/shard_map/pallas_call | solution.py:312
  21.9 0.6 %subtract_bitcast_fusion = (f32[8,320]{1,0:T(8,128)}, f32[8,320]{1,0:T(8,128)}) fusion(f32[4,8,320]{2,1,0:T(8,128)S(1)} %shard_map.104), kind=kLoop, calls=%fused_computation | loop fusion | flops 5120 | bytes 61440 | tf_op jit(solution)/shard_map/sub | solution.py:364

commit v9 on v8

--- a/solution.py
+++ b/solution.py
@@ -142,22 +142,29 @@
 
     row_ids = lax.broadcasted_iota(jnp.int32, (own, nv), 0)
 
+    wide = solved.shape[1] // own
+
     def precondition(vector):
-        rounded = vector.astype(BF16).astype(F32)
+        rounded = vector.astype(BF16)
+        total = jnp.zeros((own, nv), F32)
+        half = own // 2
+        for first in range(0, own, half):
+            for load in loads[first : first + half]:
+                load.wait()
+            every = nt(rounded, binv[first : first + half].reshape(half * nv, nv))
+            for e in range(half):
+                block = every[:, e * nv : (e + 1) * nv]
+                total += jnp.where(row_ids == first + e, block, 0.0)
+        return total
+
+    def lift_and_precondition(vector):
+        both = nn(two_terms(vector), solved[...])
+        every = both[:own] + both[own:]
         total = jnp.zeros((own, nv), F32)
         for e in range(own):
-            loads[e].wait()
-            total += nt(jnp.where(row_ids == e, rounded, 0.0).astype(BF16), binv[e])
+            block = every[:, e * wide : e * wide + nv]
+            total += jnp.where(row_ids == e, block, 0.0)
         return total
-
-    def lift_and_precondition(vector):
-        high = vector.astype(BF16).astype(F32)
-        terms = jnp.concatenate([high, vector - high], axis=0)
-        term_ids = jnp.concatenate([row_ids, row_ids], axis=0)
-        total = jnp.zeros((2 * own, nv), F32)
-        for e in range(own):
-            total += nn(jnp.where(term_ids == e, terms, 0.0).astype(BF16), solved[e])
-        return total[:own] + total[own:]
 
     def send_vector(step):
         for peer in range(n_face):
@@ -204,7 +211,9 @@
     flux_turned[...] = flux[...].T
     trace_turned[...] = trace[...].T
     for e in range(own):
-        solved[e] = nt(trace_turned[...], binv[e]).astype(BF16)
+        block = nt(trace_turned[...], binv[e])
+        block = jnp.concatenate([block, jnp.zeros((nv, wide - nv), F32)], axis=1)
+        solved[:, e * wide : (e + 1) * wide] = block.astype(BF16)
 
     send_meta.wait_recv()
     own_ids = lax.broadcasted_iota(jnp.int32, (own, slots), 0)
@@ -318,7 +327,7 @@
             pltpu.VMEM((own, nv), BF16),
             pltpu.VMEM((own, nv), F32),
             pltpu.VMEM((own, nv, nv), BF16),
-            pltpu.VMEM((own, nv, nv), BF16),
+            pltpu.VMEM((nv, own * -(-nv // LANES) * LANES), BF16),
             pltpu.VMEM((nv, nv), BF16),
             pltpu.VMEM((nv, nv), BF16),
             pltpu.VMEM((nv, nv), BF16),

time: 22.7 us -> 22.6 us (level)
  no operation moved by 1% of the time
where the time goes in v9:
time: 22.6 us; the launch traced here: 22.5 us
  Pallas kernels  20.6 us (91%)
  between operations  1.29 us (6%)
  other arithmetic  0.61 us (3%)
    pallas_call x1, Pallas kernels, on_device(): pl.pallas_call(functools.partial(kernel, n_dom, n_face), out_shape=pltpu....  20.6 us
    sub x1, other arithmetic, on_device(): return (terms[0] + terms[1], terms[2] - terms[3])  0.61 us

profile of v9, /device:TPU:0, one launch (start us, length us, event | category | flops | bytes accessed | tf_op | source)
XLA Modules:
  0.0 22.5 jit_solution(9102323851774118939)
XLA Ops:
  1.3 20.6 %shard_map.104 = f32[4,8,320]{2,1,0:T(8,128)S(1)} custom-call(bf16[8,320]{1,0:T(8,128)(2,1)} %state_hbm.1, bf16[32,320]{1,0:T(8,128)(2,1)} %metric_hbm.1, f32[8,320]{1,0:T(8,128)} %rhs_hbm.1, bf16[8,320,320]{2,1,0:T(8,128)(2,1)} %binv_hbm.1, bf16[320,320]{1,0:T(8,128)(2,1)} %trace_hbm.1, bf16[320,320]{1,0:T(8,128)(2,1)} %flux_hbm.1, s32[1,32]{1,0:T(1,128)} %bitcast.8, ...), custom_call_target="tpu_custom_call" | custom-call | tf_op jit(solution)/shard_map/pallas_call | solution.py:321
  21.9 0.6 %subtract_bitcast_fusion = (f32[8,320]{1,0:T(8,128)}, f32[8,320]{1,0:T(8,128)}) fusion(f32[4,8,320]{2,1,0:T(8,128)S(1)} %shard_map.104), kind=kLoop, calls=%fused_computation | loop fusion | flops 5120 | bytes 61440 | tf_op jit(solution)/shard_map/sub | solution.py:373

commit v10 on v9

--- a/solution.py
+++ b/solution.py
@@ -219,8 +219,7 @@
     own_ids = lax.broadcasted_iota(jnp.int32, (own, slots), 0)
     member_ids = lax.broadcasted_iota(jnp.int32, (n_face * own, slots), 0)
     pick = (member_ids == meta_in[0:1, 0:slots]).astype(F32).T.astype(BF16)
-    gather_rows = (own_ids == meta_in[1:2, 0:slots]).astype(F32)
-    gather_rows = jnp.concatenate([gather_rows, gather_rows], axis=1).astype(BF16)
+    gather_rows = (own_ids == meta_in[1:2, 0:slots]).astype(F32).astype(BF16)
 
     def picked(blocks):
         return nn(pick, blocks.astype(F32).reshape(n_face * own, nv).astype(BF16))
@@ -232,9 +231,8 @@
     def operate(step, vector):
         await_recv(vec_in.at[step], vec_send.at[step], vec_recv.at[step], (ahead, f))
         lifted = nn(picked(vec_in[step]).astype(BF16), trace[...])
-        spread = nn(two_terms(lifted * metric_in[...].astype(F32)), flux_turned[...])
-        scaled = (spread[:slots] + spread[slots:]) * speeds
-        summed = nn(gather_rows, two_terms(scaled))
+        spread = nn((lifted * metric_in[...].astype(F32)).astype(BF16), flux_turned[...])
+        summed = nn(gather_rows, (spread * speeds).astype(BF16))
         return vector + lift_and_precondition(summed)
 
     first_vec = operate(0, start_vec)

time: 22.6 us -> 22.6 us (level)
  no operation moved by 1% of the time
where the time goes in v10:
time: 22.6 us; the launch traced here: 22.4 us
  Pallas kernels  20.5 us (91%)
  between operations  1.29 us (6%)
  other arithmetic  0.61 us (3%)
    pallas_call x1, Pallas kernels, on_device(): pl.pallas_call(functools.partial(kernel, n_dom, n_face), out_shape=pltpu....  20.5 us
    sub x1, other arithmetic, on_device(): return (terms[0] + terms[1], terms[2] - terms[3])  0.61 us

profile of v10, /device:TPU:0, one launch (start us, length us, event | category | flops | bytes accessed | tf_op | source)
XLA Modules:
  0.0 22.4 jit_solution(8968577361149809606)
XLA Ops:
  1.3 20.5 %shard_map.104 = f32[4,8,320]{2,1,0:T(8,128)S(1)} custom-call(bf16[8,320]{1,0:T(8,128)(2,1)} %state_hbm.1, bf16[32,320]{1,0:T(8,128)(2,1)} %metric_hbm.1, f32[8,320]{1,0:T(8,128)} %rhs_hbm.1, bf16[8,320,320]{2,1,0:T(8,128)(2,1)} %binv_hbm.1, bf16[320,320]{1,0:T(8,128)(2,1)} %trace_hbm.1, bf16[320,320]{1,0:T(8,128)(2,1)} %flux_hbm.1, s32[1,32]{1,0:T(1,128)} %bitcast.8, ...), custom_call_target="tpu_custom_call" | custom-call | tf_op jit(solution)/shard_map/pallas_call | solution.py:319
  21.8 0.6 %subtract_bitcast_fusion = (f32[8,320]{1,0:T(8,128)}, f32[8,320]{1,0:T(8,128)}) fusion(f32[4,8,320]{2,1,0:T(8,128)S(1)} %shard_map.104), kind=kLoop, calls=%fused_computation | loop fusion | flops 5120 | bytes 61440 | tf_op jit(solution)/shard_map/sub | solution.py:371
